TPU v7x, 256 devices: a whole 4x4x8 slice. The times are simulated.
256 devices in a mesh: dp: 16 (over x, y), expert: 16 (over z, core).
Axes of the slice: x: 4, y: 4, z: 8, core: 2. Of those that a mesh axis runs over, the one named last changes fastest.
Arguments:
- tokens: bfloat16 [40960, 2048], P(('dp', 'expert')), may hold values from -6 to 6
- routes: int32 [40960, 2], P(('dp', 'expert')), may hold values from 0 to 15, all different within a row; in each aligned block of 160 rows (0 to 159, 160 to 319, ...) at most 30 rows name the same one
- route_gains: float32 [40960, 2], P(('dp', 'expert')), may hold values from 0.1 to 1
- cotangent: bfloat16 [40960, 2048], P(('dp', 'expert')), may hold values from -24 to 24
- w_gate: bfloat16 [16, 2048, 768], P('expert'), may hold values from -0.125 to 0.125
- w_up: bfloat16 [16, 2048, 768], P('expert'), may hold values from -0.125 to 0.125
- w_down: bfloat16 [16, 2048, 768], P('expert'), may hold values from -0.21875 to 0.21875
Outputs:
- layer_output: bfloat16 [40960, 2048], P(('dp', 'expert'))
- input_grad: bfloat16 [40960, 2048], P(('dp', 'expert'))
- grad_gate: bfloat16 [16, 2048, 768], P('expert', 'dp')
- grad_up: bfloat16 [16, 2048, 768], P('expert', 'dp')
- grad_down: bfloat16 [16, 2048, 768], P('expert', 'dp')
Inputs may be any that keep to these rules, and one draw needn't show every extreme that they name: `routes`: each row names 2 different experts. Within the rows of one device (aligned blocks of 160 rows) no expert is named more than 30 times, and in some device's rows one expert is named exactly 30 times.
All inputs are finite; a program needn't handle non-finite values.
Results may differ from a plain program's by a relative error of at most 0.015.
Values may be sent and summed in bfloat16 or wider, within the bound.
A program may use at most 128 MiB of HBM per device.

v0:
```python
import jax
import jax.numpy as jnp
from jax import lax
from jax.sharding import PartitionSpec as P

SLOTS = 32


def slot_masks(routes, experts):
    rows, picks = routes.shape
    chosen = routes.T.reshape(1, -1)
    labels = lax.broadcasted_iota(jnp.int32, (experts, rows * picks), 0)
    matches = chosen == labels
    total = rows * picks
    earlier = lax.broadcasted_iota(jnp.int32, (total, total), 0) < lax.broadcasted_iota(
        jnp.int32, (total, total), 1
    )
    before = jnp.dot(
        matches.astype(jnp.bfloat16),
        earlier.astype(jnp.bfloat16),
        preferred_element_type=jnp.float32,
    )
    position = jnp.sum(jnp.where(matches, before, 0.0), axis=0).astype(jnp.int32)
    target = chosen[0] * SLOTS + position
    slots = lax.broadcasted_iota(jnp.int32, (experts * SLOTS, total), 0)
    return (slots == target[None, :]).reshape(experts * SLOTS, picks, rows)


def rows_t(left, right):
    return lax.dot_general(
        left, right, (((1,), (1,)), ((), ())), preferred_element_type=jnp.float32
    )


def outer_rows(left, right):
    return lax.dot_general(
        left, right, (((0,), (0,)), ((), ())), preferred_element_type=jnp.float32
    )


def shards(tokens, routes, route_gains, cotangent, w_gate, w_up, w_down):
    experts = lax.axis_size("expert")
    groups = lax.axis_size("dp")
    width = tokens.shape[1]
    depth = width // groups
    flip = [(a * experts + b, b * experts + a) for a in range(groups) for b in range(experts)]
    mine = lax.axis_index("dp") * depth
    hidden_units = w_gate.shape[2]

    def fetch(w):
        part = lax.dynamic_slice_in_dim(w[0], mine, depth, axis=0)
        return part

    part = jnp.concatenate([fetch(w_gate), fetch(w_up), fetch(w_down)], axis=1)
    part = lax.ppermute(part, ("dp", "expert"), flip)
    full = lax.all_gather(part, "expert", axis=0, tiled=True)
    gate_mat = full[:, :hidden_units]
    up_mat = full[:, hidden_units : 2 * hidden_units]
    down_mat = full[:, 2 * hidden_units :]
    masks = slot_masks(routes, groups)
    first = masks[:, 0, :].astype(jnp.bfloat16)
    second = masks[:, 1, :].astype(jnp.bfloat16)
    both = first + second
    gains = route_gains.T
    slot_gain = jnp.sum(jnp.where(masks, gains[None], 0.0), axis=(1, 2))
    send_tok = jnp.dot(both, tokens, preferred_element_type=jnp.float32).astype(jnp.bfloat16)
    send_cot = (
        slot_gain[:, None] * jnp.dot(both, cotangent, preferred_element_type=jnp.float32)
    ).astype(jnp.bfloat16)

    def exchange(block):
        block = block.reshape(groups, SLOTS, width)
        block = lax.all_to_all(block, "dp", split_axis=0, concat_axis=0, tiled=True)
        return block.reshape(groups * SLOTS, width)

    arrived = exchange(send_tok)
    arrived_cot = exchange(send_cot)
    pre_gate = jnp.dot(arrived, gate_mat, preferred_element_type=jnp.float32)
    pre_up = jnp.dot(arrived, up_mat, preferred_element_type=jnp.float32)
    sigma = jax.nn.sigmoid(pre_gate)
    activated = pre_gate * sigma
    hidden = (activated * pre_up).astype(jnp.bfloat16)
    d_hidden = jnp.dot(arrived_cot, down_mat, preferred_element_type=jnp.float32)
    d_gate = (d_hidden * pre_up * (sigma * (1.0 + pre_gate * (1.0 - sigma)))).astype(jnp.bfloat16)
    d_up = (d_hidden * activated).astype(jnp.bfloat16)
    partial = jnp.concatenate(
        [outer_rows(arrived, d_gate), outer_rows(arrived, d_up), outer_rows(arrived_cot, hidden)],
        axis=1,
    ).astype(jnp.bfloat16)
    summed = lax.psum_scatter(partial, "expert", scatter_dimension=0, tiled=True)
    produced = rows_t(hidden, down_mat).astype(jnp.bfloat16)
    d_pick = (rows_t(d_gate, gate_mat) + rows_t(d_up, up_mat)).astype(jnp.bfloat16)
    back_out = exchange(produced)
    back_grad = exchange(d_pick)
    layer_output = (
        gains[0][:, None] * outer_rows(first, back_out)
        + gains[1][:, None] * outer_rows(second, back_out)
    ).astype(jnp.bfloat16)
    input_grad = (outer_rows(first, back_grad) + outer_rows(second, back_grad)).astype(jnp.bfloat16)
    summed = lax.ppermute(summed, ("dp", "expert"), flip)
    grad_gate = summed[None, :, :hidden_units]
    grad_up = summed[None, :, hidden_units : 2 * hidden_units]
    grad_down = summed[None, :, 2 * hidden_units :]
    return (layer_output, input_grad, grad_gate, grad_up, grad_down)


def solution(mesh):
    rows = P(("dp", "expert"), None)
    weights = P("expert", None, None)
    shares = P("expert", "dp", None)
    return jax.shard_map(
        shards,
        mesh=mesh,
        in_specs=(rows, rows, rows, rows, weights, weights, weights),
        out_specs=(rows, rows, shares, shares, shares),
        check_vma=False,
    )
```

profile of v0, /device:TPU:14, one launch (start us, length us, event | category | flops | bytes accessed | tf_op | source)
XLA Modules:
  0.0 330.9 jit_solution(815282746643636325)
XLA Ops:
  7.3 1.8 copy-done
  9.1 1.1 dynamic-slice_bitcast_fusion
  10.3 7.4 %collective-permute-start = (bf16[128,2304]{1,0:T(8,128)(2,1)S(1)}, bf16[128,2304]{1,0:T(8,128)(2,1)S(1)}, u32[]{:S(2)}, u32[]{:S(2)}) collective-permute-start(bf16[128,2304]{1,0:T(8,128)(2,1)S(1)} %pad_maximum_fusion.1), channel_id=1, source_target_pairs={{0,0},{1,16},{2,32},{3,48},{4,64},{5,80},{6,96},{7,112},{8,128},{9... | collective-permute-start | bytes 1769480 | tf_op jit(solution)/shard_map/ppermute | solution.py:55
  17.7 56.6 %collective-permute-done = bf16[128,2304]{1,0:T(8,128)(2,1)S(1)} collective-permute-done((bf16[128,2304]{1,0:T(8,128)(2,1)S(1)}, bf16[128,2304]{1,0:T(8,128)(2,1)S(1)}, u32[]{:S(2)}, u32[]{:S(2)}) %collective-permute-start) | collective-permute-done | bytes 589856 | tf_op jit(solution)/shard_map/ppermute | solution.py:55
  74.3 0.8 copy-done.8
  75.2 0.1 broadcast_in_dim.31
  75.3 0.1 eq.24
  75.4 0.2 fusion.14
  75.6 0.1 convert_element_type.48
  75.6 0.2 select_reduce_fusion
  75.8 0.2 iota_compare_fusion.1
  76.0 2.1 multiply_convert_fusion
  78.1 5.6 %all-to-all-start.2 = ((bf16[16,32,2048]{2,1,0:T(8,128)(2,1)}), bf16[16,32,2048]{2,1,0:T(8,128)(2,1)S(1)}, u32[]{:S(2)}, u32[]{:S(2)}) async-start(bf16[16,32,2048]{2,1,0:T(8,128)(2,1)} %bitcast.72), calls=%async_computation.2 | async-start | bytes 4194304 | tf_op jit(solution)/shard_map/all_to_all | solution.py:73
  83.7 2.1 convolution_convert_fusion.3
  85.8 23.9 %all-to-all-done.2 = bf16[16,32,2048]{2,1,0:T(8,128)(2,1)S(1)} async-done(((bf16[16,32,2048]{2,1,0:T(8,128)(2,1)}), bf16[16,32,2048]{2,1,0:T(8,128)(2,1)S(1)}, u32[]{:S(2)}, u32[]{:S(2)}) %all-to-all-start.2) | async-done | bytes 2097184 | tf_op jit(solution)/shard_map/all_to_all | solution.py:73
  109.6 7.3 %all-to-all-start = ((bf16[16,32,2048]{2,1,0:T(8,128)(2,1)}), bf16[16,32,2048]{2,1,0:T(8,128)(2,1)}, u32[]{:S(2)}, u32[]{:S(2)}) async-start(bf16[16,32,2048]{2,1,0:T(8,128)(2,1)} %bitcast.5), calls=%async_computation | async-start | bytes 4194304 | tf_op jit(solution)/shard_map/all_to_all | solution.py:73
  117.0 0.2 reduce-scatter.4.cloned.1.call-start
  117.2 18.1 %all-gather.2.cloned.1.call-done = bf16[2048,2304]{1,0:T(8,128)(2,1)} async-done(((bf16[128,2304]{1,0:T(8,128)(2,1)}), bf16[2048,2304]{1,0:T(8,128)(2,1)}) %all-gather.2.cloned.1.call-update) | async-done | bytes 9437200 | tf_op jit(solution)/shard_map/all_gather | solution.py:56
  135.3 4.8 %fusion = f32[512,768]{1,0:T(8,128)} fusion(bf16[512,2048]{1,0:T(8,128)(2,1)S(1)} %bitcast.68, bf16[2048,2304]{1,0:T(8,128)(2,1)} %all-gather.2.cloned.1.call-done), kind=kOutput, calls=%fused_computation.8 | convolution fusion | flops 1610612736 | bytes 6815744 | tf_op jit(solution)/shard_map/dot_general | solution.py:83
  140.1 0.1 all-to-all-done
  140.2 4.4 %fusion.5 = f32[512,768]{1,0:T(8,128)S(1)} fusion(bf16[512,2048]{1,0:T(8,128)(2,1)} %bitcast.6, bf16[2048,2304]{1,0:T(8,128)(2,1)} %all-gather.2.cloned.1.call-done), kind=kOutput, calls=%fused_computation.13 | convolution fusion | flops 1610612736 | bytes 6815744 | tf_op jit(solution)/shard_map/dot_general | solution.py:79
  144.7 5.0 %multiply_convert_fusion.2 = (bf16[512,768]{1,0:T(8,128)(2,1)S(1)}, bf16[512,768]{1,0:T(8,128)(2,1)S(1)}, bf16[512,768]{1,0:T(8,128)(2,1)S(1)}) fusion(f32[512,768]{1,0:T(8,128)S(1)} %copy-done.16, f32[512,768]{1,0:T(8,128)S(1)} %fusion.5, bf16[512,2048]{1,0:T(8,128)(2,1)} %bitcast.6, bf16[2048,2304]{1,0:T(8,128)(2,1)} %all-gather.2.cloned.1.call-done), kind=kOutput, calls=%fused_computation.25 | convolution fusion | flops 1616510976 | bytes 10747904 | tf_op jit(solution)/shard_map/dot_general | solution.py:78
  149.7 1.8 convolution_convert_fusion
  151.6 3.4 %convolution_convert_fusion.1 = bf16[2048,768]{0,1:T(8,128)(2,1)S(1)} fusion(bf16[512,2048]{1,0:T(8,128)(2,1)} %bitcast.6, bf16[512,768]{1,0:T(8,128)(2,1)S(1)} %get-tuple-element.26), kind=kOutput, calls=%fused_computation.4 | convolution fusion | flops 1612185600 | bytes 6029312 | tf_op jit(solution)/shard_map/dot_general | solution.py:36
  155.0 3.4 %convolution_convert_fusion.2 = bf16[2048,768]{0,1:T(8,128)(2,1)S(1)} fusion(bf16[512,2048]{1,0:T(8,128)(2,1)} %bitcast.6, bf16[512,768]{1,0:T(8,128)(2,1)S(1)} %get-tuple-element.25), kind=kOutput, calls=%fused_computation.5 | convolution fusion | flops 1612185600 | bytes 6029312 | tf_op jit(solution)/shard_map/dot_general | solution.py:36
  158.5 4.7 %pad_maximum_fusion = bf16[2048,2304]{0,1:T(8,128)(2,1)} fusion(bf16[2048,768]{0,1:T(8,128)(2,1)S(1)} %convolution_convert_fusion, bf16[2048,768]{0,1:T(8,128)(2,1)S(1)} %convolution_convert_fusion.1, bf16[2048,768]{0,1:T(8,128)(2,1)S(1)} %convolution_convert_fusion.2), kind=kLoop, calls=%fused_computation | loop fusion | flops 28311552 | bytes 18874368 | tf_op jit(solution)/shard_map/concatenate | solution.py:86
  163.1 12.4 %copy.25 = bf16[2048,2304]{1,0:T(8,128)(2,1)} copy(bf16[2048,2304]{0,1:T(8,128)(2,1)} %pad_maximum_fusion) | data formatting | bytes 18874368
  175.5 1.1 copy-done.15
  176.6 3.8 %fusion.3 = f32[512,2048]{1,0:T(8,128)S(1)} fusion(bf16[512,768]{1,0:T(8,128)(2,1)S(1)} %copy-done.15, bf16[2048,2304]{1,0:T(8,128)(2,1)} %all-gather.2.cloned.1.call-done), kind=kOutput, calls=%fused_computation.11 | convolution fusion | flops 1610612736 | bytes 8126464 | tf_op jit(solution)/shard_map/dot_general | solution.py:30
  180.4 5.1 %add_convert_fusion = bf16[512,2048]{1,0:T(8,128)(2,1)} fusion(f32[512,2048]{1,0:T(8,128)S(1)} %fusion.3, bf16[512,768]{1,0:T(8,128)(2,1)S(1)} %copy-done.13, bf16[2048,2304]{1,0:T(8,128)(2,1)} %all-gather.2.cloned.1.call-done), kind=kOutput, calls=%fused_computation.1 | convolution fusion | flops 1612709888 | bytes 10223616 | tf_op jit(solution)/shard_map/dot_general | solution.py:30
  185.5 8.2 %all-to-all-start.3 = ((bf16[16,32,2048]{2,1,0:T(8,128)(2,1)}), bf16[16,32,2048]{2,1,0:T(8,128)(2,1)S(1)}, u32[]{:S(2)}, u32[]{:S(2)}) async-start(bf16[16,32,2048]{2,1,0:T(8,128)(2,1)} %bitcast.71), calls=%async_computation.3 | async-start | bytes 4194304 | tf_op jit(solution)/shard_map/all_to_all | solution.py:73
  193.8 5.0 %convolution_convert_fusion.4 = bf16[512,2048]{1,0:T(8,128)(2,1)} fusion(bf16[512,768]{1,0:T(8,128)(2,1)S(1)} %copy-done.18, bf16[2048,2304]{1,0:T(8,128)(2,1)} %all-gather.2.cloned.1.call-done), kind=kOutput, calls=%fused_computation.7 | convolution fusion | flops 1611661312 | bytes 6029312 | tf_op jit(solution)/shard_map/dot_general | solution.py:30
  198.8 21.2 %all-to-all-done.3 = bf16[16,32,2048]{2,1,0:T(8,128)(2,1)S(1)} async-done(((bf16[16,32,2048]{2,1,0:T(8,128)(2,1)}), bf16[16,32,2048]{2,1,0:T(8,128)(2,1)S(1)}, u32[]{:S(2)}, u32[]{:S(2)}) %all-to-all-start.3) | async-done | bytes 2097184 | tf_op jit(solution)/shard_map/all_to_all | solution.py:73
  220.0 1.4 copy-done.3
  221.3 7.0 %all-to-all-start.1 = ((bf16[16,32,2048]{2,1,0:T(8,128)(2,1)}), bf16[16,32,2048]{2,1,0:T(8,128)(2,1)S(1)}, u32[]{:S(2)}, u32[]{:S(2)}) async-start(bf16[16,32,2048]{2,1,0:T(8,128)(2,1)} %bitcast.70), calls=%async_computation.1 | async-start | bytes 4194304 | tf_op jit(solution)/shard_map/all_to_all | solution.py:73
  228.4 2.3 fusion.15
  230.7 1.4 fusion.11
  232.1 20.1 %reduce-scatter.4.cloned.1.call-done = bf16[128,2304]{1,0:T(8,128)(2,1)} async-done(((bf16[2048,2304]{1,0:T(8,128)(2,1)}), bf16[128,2304]{1,0:T(8,128)(2,1)}) %reduce-scatter.4.cloned.1.call-update) | async-done | bytes 589840
  252.2 2.1 copy.26
  254.4 1.9 collective-permute-start.1
  256.3 1.3 copy-done.2
  257.6 0.5 convolution_multiply_fusion
  258.2 3.2 fusion.12
  261.3 57.5 %collective-permute-done.1 = bf16[128,2304]{0,1:T(8,128)(2,1)} collective-permute-done((bf16[128,2304]{0,1:T(8,128)(2,1)}, bf16[128,2304]{0,1:T(8,128)(2,1)}, u32[]{:S(2)}, u32[]{:S(2)}) %collective-permute-start.1) | collective-permute-done | bytes 589856 | tf_op jit(solution)/shard_map/ppermute | solution.py:100
  318.8 1.8 slice_bitcast_fusion.2
  320.6 1.7 copy.22
  322.4 0.8 copy.23
  323.2 0.8 copy.24
  (43 shorter events, 0.2 us)
Async XLA Ops:
  7.2 1.9 copy-start
  7.2 68.0 %copy-start.10 = (f32[160,2]{0,1:T(2,128)S(1)}, f32[160,2]{0,1:T(2,128)}, u32[]{:S(2)}) copy-start(f32[160,2]{0,1:T(2,128)} %param.9) | copy-start | bytes 3844
  7.2 68.1 %copy-start.9 = (s32[160,2]{0,1:T(2,128)S(1)}, s32[160,2]{0,1:T(2,128)}, u32[]{:S(2)}) copy-start(s32[160,2]{0,1:T(2,128)} %param.8) | copy-start | bytes 3844
  7.2 128.1 %all-gather.2.cloned.1.call-start = ((), (), s32[]{:S(2)}) async-start(), calls=%async_computation.5 | async-start | bytes 10027008 | tf_op jit(solution)/shard_map/all_gather | solution.py:56
  9.1 66.9 %copy-start.11 = (bf16[160,2048]{1,0:T(8,128)(2,1)S(1)}, bf16[160,2048]{1,0:T(8,128)(2,1)}, u32[]{:S(2)}) copy-start(bf16[160,2048]{1,0:T(8,128)(2,1)} %param.10) | copy-start | bytes 1966084
  10.3 64.1 %collective-permute-start = (bf16[128,2304]{1,0:T(8,128)(2,1)S(1)}, bf16[128,2304]{1,0:T(8,128)(2,1)S(1)}, u32[]{:S(2)}, u32[]{:S(2)}) collective-permute-start(bf16[128,2304]{1,0:T(8,128)(2,1)S(1)} %pad_maximum_fusion.1), channel_id=1, source_target_pairs={{0,0},{1,16},{2,32},{3,48},{4,64},{5,80},{6,96},{7,112},{8,128},{9... | collective-permute-start | bytes 1769480 | tf_op jit(solution)/shard_map/ppermute | solution.py:55
  74.3 0.8 copy-start.8
  78.1 5.6 %copy-start.7 = (bf16[160,2048]{1,0:T(8,128)(2,1)S(1)}, bf16[160,2048]{1,0:T(8,128)(2,1)}, u32[]{:S(2)}) copy-start(bf16[160,2048]{1,0:T(8,128)(2,1)} %param.7) | copy-start | bytes 1966084
  78.1 31.5 %all-to-all-start.2 = ((bf16[16,32,2048]{2,1,0:T(8,128)(2,1)}), bf16[16,32,2048]{2,1,0:T(8,128)(2,1)S(1)}, u32[]{:S(2)}, u32[]{:S(2)}) async-start(bf16[16,32,2048]{2,1,0:T(8,128)(2,1)} %bitcast.72), calls=%async_computation.2 | async-start | bytes 4194304 | tf_op jit(solution)/shard_map/all_to_all | solution.py:73
  109.6 25.7 %copy-start.5 = (bf16[16,32,2048]{2,1,0:T(8,128)(2,1)}, bf16[16,32,2048]{2,1,0:T(8,128)(2,1)S(1)}, u32[]{:S(2)}) copy-start(bf16[16,32,2048]{2,1,0:T(8,128)(2,1)S(1)} %all-to-all-done.2) | copy-start | bytes 6291460
  109.6 30.6 %all-to-all-start = ((bf16[16,32,2048]{2,1,0:T(8,128)(2,1)}), bf16[16,32,2048]{2,1,0:T(8,128)(2,1)}, u32[]{:S(2)}, u32[]{:S(2)}) async-start(bf16[16,32,2048]{2,1,0:T(8,128)(2,1)} %bitcast.5), calls=%async_computation | async-start | bytes 4194304 | tf_op jit(solution)/shard_map/all_to_all | solution.py:73
  117.0 135.2 %reduce-scatter.4.cloned.1.call-start = ((), (), s32[]{:S(2)}) async-start(), calls=%async_computation.6 | async-start | bytes 10027008
  140.2 4.4 %copy-start.16 = (f32[512,768]{1,0:T(8,128)S(1)}, f32[512,768]{1,0:T(8,128)}, u32[]{:S(2)}) copy-start(f32[512,768]{1,0:T(8,128)} %fusion) | copy-start | bytes 4718596
  144.7 5.0 %copy-start.6 = (bf16[16,32,2048]{2,1,0:T(8,128)(2,1)S(1)}, bf16[16,32,2048]{2,1,0:T(8,128)(2,1)}, u32[]{:S(2)}) copy-start(bf16[16,32,2048]{2,1,0:T(8,128)(2,1)} %copy-done.5) | copy-start | bytes 6291460
  149.7 1.9 copy-start.17
  149.7 1.9 copy-start.14
  149.7 5.3 %copy-start.12 = (bf16[512,768]{1,0:T(8,128)(2,1)}, bf16[512,768]{1,0:T(8,128)(2,1)S(1)}, u32[]{:S(2)}) copy-start(bf16[512,768]{1,0:T(8,128)(2,1)S(1)} %get-tuple-element.25) | copy-start | bytes 2359300
  175.5 1.1 copy-start.15
  176.6 3.8 %copy-start.13 = (bf16[512,768]{1,0:T(8,128)(2,1)S(1)}, bf16[512,768]{1,0:T(8,128)(2,1)}, u32[]{:S(2)}) copy-start(bf16[512,768]{1,0:T(8,128)(2,1)} %copy-done.12) | copy-start | bytes 2359300
  185.5 8.3 %copy-start.18 = (bf16[512,768]{1,0:T(8,128)(2,1)S(1)}, bf16[512,768]{1,0:T(8,128)(2,1)}, u32[]{:S(2)}) copy-start(bf16[512,768]{1,0:T(8,128)(2,1)} %copy-done.17) | copy-start | bytes 2359300
  185.5 34.5 %all-to-all-start.3 = ((bf16[16,32,2048]{2,1,0:T(8,128)(2,1)}), bf16[16,32,2048]{2,1,0:T(8,128)(2,1)S(1)}, u32[]{:S(2)}, u32[]{:S(2)}) async-start(bf16[16,32,2048]{2,1,0:T(8,128)(2,1)} %bitcast.71), calls=%async_computation.3 | async-start | bytes 4194304 | tf_op jit(solution)/shard_map/all_to_all | solution.py:73
  220.0 1.4 copy-start.3
  221.3 34.9 %all-to-all-start.1 = ((bf16[16,32,2048]{2,1,0:T(8,128)(2,1)}), bf16[16,32,2048]{2,1,0:T(8,128)(2,1)S(1)}, u32[]{:S(2)}, u32[]{:S(2)}) async-start(bf16[16,32,2048]{2,1,0:T(8,128)(2,1)} %bitcast.70), calls=%async_computation.1 | async-start | bytes 4194304 | tf_op jit(solution)/shard_map/all_to_all | solution.py:73
  228.4 2.4 copy-start.4
  254.4 64.5 %collective-permute-start.1 = (bf16[128,2304]{0,1:T(8,128)(2,1)}, bf16[128,2304]{0,1:T(8,128)(2,1)}, u32[]{:S(2)}, u32[]{:S(2)}) collective-permute-start(bf16[128,2304]{0,1:T(8,128)(2,1)} %copy.26), channel_id=1, source_target_pairs={{0,0},{1,16},{2,32},{3,48},{4,64},{5,80},{6,96},{7,112},{8,128},{9... | collective-permute-start | bytes 1769480 | tf_op jit(solution)/shard_map/ppermute | solution.py:100
  256.3 1.4 copy-start.2
  258.2 65.9 %copy-start.1 = (bf16[1,2048,768]{2,1,0:T(8,128)(2,1)S(1)}, bf16[1,2048,768]{2,1,0:T(8,128)(2,1)}, u32[]{:S(2)}) copy-start(bf16[1,2048,768]{2,1,0:T(8,128)(2,1)} %param.11) | copy-start | bytes 9437188
Sparse Core Ops, SparseCore 0:
  75.3 59.9 all-gather.1
  175.6 76.5 reduce-scatter.3
where the time goes:
time: 332 us; the launch traced here: 331 us
  waiting for transfers between devices  198 us (60%)
  matrix products  48.6 us (15%)
  starting transfers between devices  37.8 us (11%)
  local copies, waits for them, and re-layouts  27.6 us (8%)
  between operations  14.3 us (4%)
  other arithmetic  5.04 us (2%)
    ppermute x1, waiting for transfers between devices, shards(): summed = lax.ppermute(summed, ('dp', 'expert'), flip)  57.5 us
    ppermute x1, waiting for transfers between devices, shards(): part = lax.ppermute(part, ('dp', 'expert'), flip)  56.6 us
    all_to_all x4, waiting for transfers between devices, exchange(): block = lax.all_to_all(block, 'dp', split_axis=0, concat_axis=0, tiled=True)  45.1 us
    all_to_all x4, starting transfers between devices, exchange(): block = lax.all_to_all(block, 'dp', split_axis=0, concat_axis=0, tiled=True)  28.2 us
    unnamed x43, local copies, waits for them, and re-layouts  24.4 us
    unnamed x3, waiting for transfers between devices  20.2 us
    all_gather x1, waiting for transfers between devices, shards(): full = lax.all_gather(part, 'expert', axis=0, tiled=True)  18.1 us
    dot_general x7, matrix products, outer_rows(): lax.dot_general(left, right, (((0,), (0,)), ((), ())), preferred_element_...  16.1 us
  transfers between devices with their start and end apart: 8, of which 7 were waited for; matrix products, arithmetic and copies ran while one was open for 10% of the time, Pallas kernels for 0%

commit v1 on v0

--- a/solution.py
+++ b/solution.py
@@ -39,6 +39,20 @@
 
 
 def shards(tokens, routes, route_gains, cotangent, w_gate, w_up, w_down):
+
+    def _take_strings(view, ax_name):
+        n_shards = lax.axis_size(ax_name)
+        current_value = view
+        nodes = [current_value]
+        known = [(u - 1, u) for u in range(1, n_shards)] + [(n_shards - 1, 0)]
+        for _ in range(n_shards - 1):
+            current_value = lax.ppermute(current_value, ax_name, known)
+            nodes += [current_value]
+        x_now = jnp.concatenate([*reversed(nodes)], axis=0)
+        heard = lax.axis_index(ax_name)
+        w_next = jnp.roll(x_now, (heard + 1) * current_value.shape[0], axis=0)
+        return w_next
+
     experts = lax.axis_size("expert")
     groups = lax.axis_size("dp")
     width = tokens.shape[1]
@@ -53,7 +67,7 @@
 
     part = jnp.concatenate([fetch(w_gate), fetch(w_up), fetch(w_down)], axis=1)
     part = lax.ppermute(part, ("dp", "expert"), flip)
-    full = lax.all_gather(part, "expert", axis=0, tiled=True)
+    full = _take_strings(part, "expert")
     gate_mat = full[:, :hidden_units]
     up_mat = full[:, hidden_units : 2 * hidden_units]
     down_mat = full[:, 2 * hidden_units :]

time: 332 us -> 499 us (1.50)
  waiting for transfers between devices: 198 us -> 311 us
  local copies, waits for them, and re-layouts: 27.6 us -> 69.3 us
  matrix products: 48.6 us -> 54.6 us
    ppermute x0 -> x15, waiting for transfers between devices: none -> 143 us  [_take_strings(): current_value = lax.ppermute(current_value, ax_name, known)]
    unnamed x43 -> x84, local copies, waits for them, and re-layouts: 24.4 us -> 64.6 us
    all_to_all x4, waiting for transfers between devices: 45.1 us -> 22.6 us  [exchange(): block = lax.all_to_all(block, 'dp', split_axis=0, concat_axis=0, tiled=True)]
    all_gather x1 -> x0, waiting for transfers between devices: 18.1 us -> none  [shards(): full = lax.all_gather(part, 'expert', axis=0, tiled=True)]
    unnamed x3 -> x2, waiting for transfers between devices: 20.2 us -> 30.9 us
  transfers between devices with their start and end apart: 8 -> 22, of which waited for: 7 -> 19; matrix products, arithmetic and copies ran while one was open for 10% -> 15% of each run, Pallas kernels for 0% -> 0%
where the time goes in v1:
time: 499 us; the launch traced here: 497 us
  waiting for transfers between devices  311 us (62%)
  local copies, waits for them, and re-layouts  69.3 us (14%)
  matrix products  54.6 us (11%)
  starting transfers between devices  42 us (8%)
  between operations  14.3 us (3%)
  other arithmetic  5.83 us (1%)
    ppermute x15, waiting for transfers between devices, _take_strings(): current_value = lax.ppermute(current_value, ax_name, known)  143 us
    unnamed x84, local copies, waits for them, and re-layouts  64.6 us
    ppermute x1, waiting for transfers between devices, shards(): summed = lax.ppermute(summed, ('dp', 'expert'), flip)  57.5 us
    ppermute x1, waiting for transfers between devices, shards(): part = lax.ppermute(part, ('dp', 'expert'), flip)  56.6 us
    all_to_all x4, starting transfers between devices, exchange(): block = lax.all_to_all(block, 'dp', split_axis=0, concat_axis=0, tiled=True)  32.4 us
    unnamed x2, waiting for transfers between devices  30.9 us
    all_to_all x4, waiting for transfers between devices, exchange(): block = lax.all_to_all(block, 'dp', split_axis=0, concat_axis=0, tiled=True)  22.6 us
    dot_general x7, matrix products, outer_rows(): lax.dot_general(left, right, (((0,), (0,)), ((), ())), preferred_element_...  19.9 us
  transfers between devices with their start and end apart: 22, of which 19 were waited for; matrix products, arithmetic and copies ran while one was open for 15% of the time, Pallas kernels for 0%

profile of v1, /device:TPU:14, one launch (start us, length us, event | category | flops | bytes accessed | tf_op | source)
XLA Modules:
  0.0 497.0 jit_solution(16677216725485037382)
XLA Ops:
  10.2 7.4 %collective-permute-start = (bf16[128,2304]{1,0:T(8,128)(2,1)S(1)}, bf16[128,2304]{1,0:T(8,128)(2,1)S(1)}, u32[]{:S(2)}, u32[]{:S(2)}) collective-permute-start(bf16[128,2304]{1,0:T(8,128)(2,1)S(1)} %pad_maximum_fusion.1), channel_id=1, source_target_pairs={{0,0},{1,16},{2,32},{3,48},{4,64},{5,80},{6,96},{7,112},{8,128},{9... | collective-permute-start | bytes 1769480 | tf_op jit(solution)/shard_map/ppermute | solution.py:69
  17.6 56.6 %collective-permute-done = bf16[128,2304]{1,0:T(8,128)(2,1)S(1)} collective-permute-done((bf16[128,2304]{1,0:T(8,128)(2,1)S(1)}, bf16[128,2304]{1,0:T(8,128)(2,1)S(1)}, u32[]{:S(2)}, u32[]{:S(2)}) %collective-permute-start) | collective-permute-done | bytes 589856 | tf_op jit(solution)/shard_map/ppermute | solution.py:69
  74.3 10.5 %collective-permute-done.1 = bf16[128,2304]{1,0:T(8,128)(2,1)S(1)} collective-permute-done((bf16[128,2304]{1,0:T(8,128)(2,1)S(1)}, bf16[128,2304]{1,0:T(8,128)(2,1)S(1)}, u32[]{:S(2)}, u32[]{:S(2)}) %collective-permute-start.1) | collective-permute-done | bytes 589856 | tf_op jit(solution)/shard_map/ppermute | solution.py:49
  84.8 10.5 %collective-permute-done.2 = bf16[128,2304]{1,0:T(8,128)(2,1)S(1)} collective-permute-done((bf16[128,2304]{1,0:T(8,128)(2,1)S(1)}, bf16[128,2304]{1,0:T(8,128)(2,1)S(1)}, u32[]{:S(2)}, u32[]{:S(2)}) %collective-permute-start.2) | collective-permute-done | bytes 589856 | tf_op jit(solution)/shard_map/ppermute | solution.py:49
  95.3 10.5 %collective-permute-done.3 = bf16[128,2304]{1,0:T(8,128)(2,1)S(1)} collective-permute-done((bf16[128,2304]{1,0:T(8,128)(2,1)S(1)}, bf16[128,2304]{1,0:T(8,128)(2,1)S(1)}, u32[]{:S(2)}, u32[]{:S(2)}) %collective-permute-start.3) | collective-permute-done | bytes 589856 | tf_op jit(solution)/shard_map/ppermute | solution.py:49
  105.8 10.5 %collective-permute-done.4 = bf16[128,2304]{1,0:T(8,128)(2,1)S(1)} collective-permute-done((bf16[128,2304]{1,0:T(8,128)(2,1)S(1)}, bf16[128,2304]{1,0:T(8,128)(2,1)S(1)}, u32[]{:S(2)}, u32[]{:S(2)}) %collective-permute-start.4) | collective-permute-done | bytes 589856 | tf_op jit(solution)/shard_map/ppermute | solution.py:49
  116.4 10.5 %collective-permute-done.5 = bf16[128,2304]{1,0:T(8,128)(2,1)S(1)} collective-permute-done((bf16[128,2304]{1,0:T(8,128)(2,1)S(1)}, bf16[128,2304]{1,0:T(8,128)(2,1)S(1)}, u32[]{:S(2)}, u32[]{:S(2)}) %collective-permute-start.5) | collective-permute-done | bytes 589856 | tf_op jit(solution)/shard_map/ppermute | solution.py:49
  127.7 10.5 %collective-permute-done.6 = bf16[128,2304]{1,0:T(8,128)(2,1)S(1)} collective-permute-done((bf16[128,2304]{1,0:T(8,128)(2,1)S(1)}, bf16[128,2304]{1,0:T(8,128)(2,1)S(1)}, u32[]{:S(2)}, u32[]{:S(2)}) %collective-permute-start.6) | collective-permute-done | bytes 589856 | tf_op jit(solution)/shard_map/ppermute | solution.py:49
  139.1 10.5 %collective-permute-done.7 = bf16[128,2304]{1,0:T(8,128)(2,1)S(1)} collective-permute-done((bf16[128,2304]{1,0:T(8,128)(2,1)S(1)}, bf16[128,2304]{1,0:T(8,128)(2,1)S(1)}, u32[]{:S(2)}, u32[]{:S(2)}) %collective-permute-start.7) | collective-permute-done | bytes 589856 | tf_op jit(solution)/shard_map/ppermute | solution.py:49
  150.4 10.5 %collective-permute-done.8 = bf16[128,2304]{1,0:T(8,128)(2,1)S(1)} collective-permute-done((bf16[128,2304]{1,0:T(8,128)(2,1)S(1)}, bf16[128,2304]{1,0:T(8,128)(2,1)S(1)}, u32[]{:S(2)}, u32[]{:S(2)}) %collective-permute-start.8) | collective-permute-done | bytes 589856 | tf_op jit(solution)/shard_map/ppermute | solution.py:49
  161.8 10.5 %collective-permute-done.9 = bf16[128,2304]{1,0:T(8,128)(2,1)S(1)} collective-permute-done((bf16[128,2304]{1,0:T(8,128)(2,1)S(1)}, bf16[128,2304]{1,0:T(8,128)(2,1)S(1)}, u32[]{:S(2)}, u32[]{:S(2)}) %collective-permute-start.9) | collective-permute-done | bytes 589856 | tf_op jit(solution)/shard_map/ppermute | solution.py:49
  173.1 10.5 %collective-permute-done.10 = bf16[128,2304]{1,0:T(8,128)(2,1)S(1)} collective-permute-done((bf16[128,2304]{1,0:T(8,128)(2,1)S(1)}, bf16[128,2304]{1,0:T(8,128)(2,1)S(1)}, u32[]{:S(2)}, u32[]{:S(2)}) %collective-permute-start.10) | collective-permute-done | bytes 589856 | tf_op jit(solution)/shard_map/ppermute | solution.py:49
  184.4 10.5 %collective-permute-done.11 = bf16[128,2304]{1,0:T(8,128)(2,1)S(1)} collective-permute-done((bf16[128,2304]{1,0:T(8,128)(2,1)S(1)}, bf16[128,2304]{1,0:T(8,128)(2,1)S(1)}, u32[]{:S(2)}, u32[]{:S(2)}) %collective-permute-start.11) | collective-permute-done | bytes 589856 | tf_op jit(solution)/shard_map/ppermute | solution.py:49
  195.8 10.6 %collective-permute-done.12 = bf16[128,2304]{1,0:T(8,128)(2,1)} collective-permute-done((bf16[128,2304]{1,0:T(8,128)(2,1)S(1)}, bf16[128,2304]{1,0:T(8,128)(2,1)}, u32[]{:S(2)}, u32[]{:S(2)}) %collective-permute-start.12) | collective-permute-done | bytes 589856 | tf_op jit(solution)/shard_map/ppermute | solution.py:49
  207.4 9.8 %collective-permute-done.13 = bf16[128,2304]{1,0:T(8,128)(2,1)} collective-permute-done((bf16[128,2304]{1,0:T(8,128)(2,1)}, bf16[128,2304]{1,0:T(8,128)(2,1)}, u32[]{:S(2)}, u32[]{:S(2)}) %collective-permute-start.13) | collective-permute-done | bytes 589856 | tf_op jit(solution)/shard_map/ppermute | solution.py:49
  218.1 3.3 convolution_convert_fusion.3
  221.4 6.9 %all-to-all-start = ((bf16[16,32,2048]{2,1,0:T(8,128)(2,1)}), bf16[16,32,2048]{2,1,0:T(8,128)(2,1)}, u32[]{:S(2)}, u32[]{:S(2)}) async-start(bf16[16,32,2048]{2,1,0:T(8,128)(2,1)} %bitcast.5), calls=%async_computation | async-start | bytes 4194304 | tf_op jit(solution)/shard_map/all_to_all | solution.py:87
  228.5 3.3 multiply_convert_fusion
  231.9 7.2 %collective-permute-done.15 = bf16[128,2304]{1,0:T(8,128)(2,1)S(1)} collective-permute-done((bf16[128,2304]{1,0:T(8,128)(2,1)}, bf16[128,2304]{1,0:T(8,128)(2,1)S(1)}, u32[]{:S(2)}, u32[]{:S(2)}) %collective-permute-start.15) | collective-permute-done | bytes 589856 | tf_op jit(solution)/shard_map/ppermute | solution.py:49
  239.9 1.9 constant_dynamic-update-slice_fusion.30
  243.8 1.9 constant_dynamic-update-slice_fusion.28
  249.5 1.9 constant_dynamic-update-slice_fusion.25
  251.5 1.9 constant_dynamic-update-slice_fusion.24
  261.3 1.9 constant_dynamic-update-slice_fusion.14
  263.3 1.9 constant_dynamic-update-slice_fusion.13
  265.2 1.9 constant_dynamic-update-slice_fusion.12
  273.2 7.2 %all-to-all-start.2 = ((bf16[16,32,2048]{2,1,0:T(8,128)(2,1)}), bf16[16,32,2048]{2,1,0:T(8,128)(2,1)}, u32[]{:S(2)}, u32[]{:S(2)}) async-start(bf16[16,32,2048]{2,1,0:T(8,128)(2,1)} %bitcast.66), calls=%async_computation.2 | async-start | bytes 4194304 | tf_op jit(solution)/shard_map/all_to_all | solution.py:87
  284.9 4.3 fusion.8
  289.3 10.1 %all-to-all-done.2 = bf16[16,32,2048]{2,1,0:T(8,128)(2,1)} async-done(((bf16[16,32,2048]{2,1,0:T(8,128)(2,1)}), bf16[16,32,2048]{2,1,0:T(8,128)(2,1)}, u32[]{:S(2)}, u32[]{:S(2)}) %all-to-all-start.2) | async-done | bytes 2097184 | tf_op jit(solution)/shard_map/all_to_all | solution.py:87
  299.4 4.3 fusion.3
  303.7 4.8 multiply_convert_fusion.2
  308.5 4.3 convolution_convert_fusion
  312.8 3.4 convolution_convert_fusion.1
  316.3 3.4 convolution_convert_fusion.2
  319.7 4.8 pad_maximum_fusion
  324.5 12.8 %copy.25 = bf16[2048,2304]{1,0:T(8,128)(2,1)} copy(bf16[2048,2304]{0,1:T(8,128)(2,1)} %pad_maximum_fusion) | data formatting | bytes 18874368
  338.4 3.8 fusion.6
  342.2 5.1 %add_convert_fusion = bf16[512,2048]{1,0:T(8,128)(2,1)} fusion(f32[512,2048]{1,0:T(8,128)S(1)} %fusion.6, bf16[512,768]{1,0:T(8,128)(2,1)S(1)} %copy-done.21, bf16[4096,2304]{1,0:T(8,128)(2,1)} %constant_dynamic-update-slice_fusion, s32[]{:T(128)S(6)} %select_n.30), kind=kOutput, calls=%fused_computation.1 | convolution fusion | flops 1612709888 | bytes 10223620 | tf_op jit(solution)/shard_map/dot_general | solution.py:30
  347.3 7.6 %all-to-all-start.3 = ((bf16[16,32,2048]{2,1,0:T(8,128)(2,1)}), bf16[16,32,2048]{2,1,0:T(8,128)(2,1)S(1)}, u32[]{:S(2)}, u32[]{:S(2)}) async-start(bf16[16,32,2048]{2,1,0:T(8,128)(2,1)} %bitcast.68), calls=%async_computation.3 | async-start | bytes 4194304 | tf_op jit(solution)/shard_map/all_to_all | solution.py:87
  354.9 5.5 %convolution_convert_fusion.4 = bf16[512,2048]{1,0:T(8,128)(2,1)} fusion(bf16[512,768]{1,0:T(8,128)(2,1)S(1)} %copy-done.23, bf16[4096,2304]{1,0:T(8,128)(2,1)} %constant_dynamic-update-slice_fusion, s32[]{:T(128)S(6)} %select_n.30, s32[]{:T(128)S(6)} %add.61), kind=kOutput, calls=%fused_computation.7 | convolution fusion | flops 1611661312 | bytes 6029320 | tf_op jit(solution)/shard_map/dot_general | solution.py:30
  360.4 12.5 %all-to-all-done.3 = bf16[16,32,2048]{2,1,0:T(8,128)(2,1)S(1)} async-done(((bf16[16,32,2048]{2,1,0:T(8,128)(2,1)}), bf16[16,32,2048]{2,1,0:T(8,128)(2,1)S(1)}, u32[]{:S(2)}, u32[]{:S(2)}) %all-to-all-start.3) | async-done | bytes 2097184 | tf_op jit(solution)/shard_map/all_to_all | solution.py:87
  372.9 10.7 %all-to-all-start.1 = ((bf16[16,32,2048]{2,1,0:T(8,128)(2,1)}), bf16[16,32,2048]{2,1,0:T(8,128)(2,1)}, u32[]{:S(2)}, u32[]{:S(2)}) async-start(bf16[16,32,2048]{2,1,0:T(8,128)(2,1)} %bitcast.67), calls=%async_computation.1 | async-start | bytes 4194304 | tf_op jit(solution)/shard_map/all_to_all | solution.py:87
  384.2 3.1 fusion.11
  387.3 30.9 %reduce-scatter.4.cloned.1.call-done = bf16[128,2304]{1,0:T(8,128)(2,1)} async-done(((bf16[2048,2304]{1,0:T(8,128)(2,1)}), bf16[128,2304]{1,0:T(8,128)(2,1)}) %reduce-scatter.4.cloned.1.call-update) | async-done | bytes 589840
  418.2 2.1 copy.26
  422.3 2.1 convolution_multiply_fusion
  424.4 3.0 fusion.12
  427.4 57.5 %collective-permute-done.16 = bf16[128,2304]{0,1:T(8,128)(2,1)} collective-permute-done((bf16[128,2304]{0,1:T(8,128)(2,1)}, bf16[128,2304]{0,1:T(8,128)(2,1)}, u32[]{:S(2)}, u32[]{:S(2)}) %collective-permute-start.16) | collective-permute-done | bytes 589856 | tf_op jit(solution)/shard_map/ppermute | solution.py:114
  (112 shorter events, 44.9 us)
Async XLA Ops:
  7.2 1.9 copy-start
  7.2 221.1 %copy-start.19 = (f32[160,2]{0,1:T(2,128)S(1)}, f32[160,2]{0,1:T(2,128)}, u32[]{:S(2)}) copy-start(f32[160,2]{0,1:T(2,128)} %param.9) | copy-start | bytes 3844
  10.2 64.1 %collective-permute-start = (bf16[128,2304]{1,0:T(8,128)(2,1)S(1)}, bf16[128,2304]{1,0:T(8,128)(2,1)S(1)}, u32[]{:S(2)}, u32[]{:S(2)}) collective-permute-start(bf16[128,2304]{1,0:T(8,128)(2,1)S(1)} %pad_maximum_fusion.1), channel_id=1, source_target_pairs={{0,0},{1,16},{2,32},{3,48},{4,64},{5,80},{6,96},{7,112},{8,128},{9... | collective-permute-start | bytes 1769480 | tf_op jit(solution)/shard_map/ppermute | solution.py:69
  74.3 10.5 %collective-permute-start.1 = (bf16[128,2304]{1,0:T(8,128)(2,1)S(1)}, bf16[128,2304]{1,0:T(8,128)(2,1)S(1)}, u32[]{:S(2)}, u32[]{:S(2)}) collective-permute-start(bf16[128,2304]{1,0:T(8,128)(2,1)S(1)} %collective-permute-done), channel_id=1, source_target_pairs={{0,1},{1,2},{2,3},{3,4},{4,5},{5,6},{6,7},{7,8},{8,9},{9,10},{10,1... | collective-permute-start | bytes 1769480 | tf_op jit(solution)/shard_map/ppermute | solution.py:49
  84.8 10.5 %collective-permute-start.2 = (bf16[128,2304]{1,0:T(8,128)(2,1)S(1)}, bf16[128,2304]{1,0:T(8,128)(2,1)S(1)}, u32[]{:S(2)}, u32[]{:S(2)}) collective-permute-start(bf16[128,2304]{1,0:T(8,128)(2,1)S(1)} %collective-permute-done.1), channel_id=1, source_target_pairs={{0,1},{1,2},{2,3},{3,4},{4,5},{5,6},{6,7},{7,8},{8,9},{9,10},{10,1... | collective-permute-start | bytes 1769480 | tf_op jit(solution)/shard_map/ppermute | solution.py:49
  95.3 10.5 %collective-permute-start.3 = (bf16[128,2304]{1,0:T(8,128)(2,1)S(1)}, bf16[128,2304]{1,0:T(8,128)(2,1)S(1)}, u32[]{:S(2)}, u32[]{:S(2)}) collective-permute-start(bf16[128,2304]{1,0:T(8,128)(2,1)S(1)} %collective-permute-done.2), channel_id=1, source_target_pairs={{0,1},{1,2},{2,3},{3,4},{4,5},{5,6},{6,7},{7,8},{8,9},{9,10},{10,1... | collective-permute-start | bytes 1769480 | tf_op jit(solution)/shard_map/ppermute | solution.py:49
  105.8 10.5 %collective-permute-start.4 = (bf16[128,2304]{1,0:T(8,128)(2,1)S(1)}, bf16[128,2304]{1,0:T(8,128)(2,1)S(1)}, u32[]{:S(2)}, u32[]{:S(2)}) collective-permute-start(bf16[128,2304]{1,0:T(8,128)(2,1)S(1)} %collective-permute-done.3), channel_id=1, source_target_pairs={{0,1},{1,2},{2,3},{3,4},{4,5},{5,6},{6,7},{7,8},{8,9},{9,10},{10,1... | collective-permute-start | bytes 1769480 | tf_op jit(solution)/shard_map/ppermute | solution.py:49
  116.4 10.5 %collective-permute-start.5 = (bf16[128,2304]{1,0:T(8,128)(2,1)S(1)}, bf16[128,2304]{1,0:T(8,128)(2,1)S(1)}, u32[]{:S(2)}, u32[]{:S(2)}) collective-permute-start(bf16[128,2304]{1,0:T(8,128)(2,1)S(1)} %collective-permute-done.4), channel_id=1, source_target_pairs={{0,1},{1,2},{2,3},{3,4},{4,5},{5,6},{6,7},{7,8},{8,9},{9,10},{10,1... | collective-permute-start | bytes 1769480 | tf_op jit(solution)/shard_map/ppermute | solution.py:49
  126.9 0.8 copy-start.3
  127.7 10.5 %collective-permute-start.6 = (bf16[128,2304]{1,0:T(8,128)(2,1)S(1)}, bf16[128,2304]{1,0:T(8,128)(2,1)S(1)}, u32[]{:S(2)}, u32[]{:S(2)}) collective-permute-start(bf16[128,2304]{1,0:T(8,128)(2,1)S(1)} %collective-permute-done.5), channel_id=1, source_target_pairs={{0,1},{1,2},{2,3},{3,4},{4,5},{5,6},{6,7},{7,8},{8,9},{9,10},{10,1... | collective-permute-start | bytes 1769480 | tf_op jit(solution)/shard_map/ppermute | solution.py:49
  138.2 0.8 copy-start.5
  139.1 10.5 %collective-permute-start.7 = (bf16[128,2304]{1,0:T(8,128)(2,1)S(1)}, bf16[128,2304]{1,0:T(8,128)(2,1)S(1)}, u32[]{:S(2)}, u32[]{:S(2)}) collective-permute-start(bf16[128,2304]{1,0:T(8,128)(2,1)S(1)} %collective-permute-done.6), channel_id=1, source_target_pairs={{0,1},{1,2},{2,3},{3,4},{4,5},{5,6},{6,7},{7,8},{8,9},{9,10},{10,1... | collective-permute-start | bytes 1769480 | tf_op jit(solution)/shard_map/ppermute | solution.py:49
  149.6 0.8 copy-start.7
  150.4 10.5 %collective-permute-start.8 = (bf16[128,2304]{1,0:T(8,128)(2,1)S(1)}, bf16[128,2304]{1,0:T(8,128)(2,1)S(1)}, u32[]{:S(2)}, u32[]{:S(2)}) collective-permute-start(bf16[128,2304]{1,0:T(8,128)(2,1)S(1)} %collective-permute-done.7), channel_id=1, source_target_pairs={{0,1},{1,2},{2,3},{3,4},{4,5},{5,6},{6,7},{7,8},{8,9},{9,10},{10,1... | collective-permute-start | bytes 1769480 | tf_op jit(solution)/shard_map/ppermute | solution.py:49
  160.9 0.8 copy-start.9
  161.8 10.5 %collective-permute-start.9 = (bf16[128,2304]{1,0:T(8,128)(2,1)S(1)}, bf16[128,2304]{1,0:T(8,128)(2,1)S(1)}, u32[]{:S(2)}, u32[]{:S(2)}) collective-permute-start(bf16[128,2304]{1,0:T(8,128)(2,1)S(1)} %collective-permute-done.8), channel_id=1, source_target_pairs={{0,1},{1,2},{2,3},{3,4},{4,5},{5,6},{6,7},{7,8},{8,9},{9,10},{10,1... | collective-permute-start | bytes 1769480 | tf_op jit(solution)/shard_map/ppermute | solution.py:49
  172.3 0.8 copy-start.11
  173.1 10.5 %collective-permute-start.10 = (bf16[128,2304]{1,0:T(8,128)(2,1)S(1)}, bf16[128,2304]{1,0:T(8,128)(2,1)S(1)}, u32[]{:S(2)}, u32[]{:S(2)}) collective-permute-start(bf16[128,2304]{1,0:T(8,128)(2,1)S(1)} %collective-permute-done.9), channel_id=1, source_target_pairs={{0,1},{1,2},{2,3},{3,4},{4,5},{5,6},{6,7},{7,8},{8,9},{9,10},{10,1... | collective-permute-start | bytes 1769480 | tf_op jit(solution)/shard_map/ppermute | solution.py:49
  183.6 0.8 copy-start.13
  184.4 10.5 %collective-permute-start.11 = (bf16[128,2304]{1,0:T(8,128)(2,1)S(1)}, bf16[128,2304]{1,0:T(8,128)(2,1)S(1)}, u32[]{:S(2)}, u32[]{:S(2)}) collective-permute-start(bf16[128,2304]{1,0:T(8,128)(2,1)S(1)} %collective-permute-done.10), channel_id=1, source_target_pairs={{0,1},{1,2},{2,3},{3,4},{4,5},{5,6},{6,7},{7,8},{8,9},{9,10},{10,1... | collective-permute-start | bytes 1769480 | tf_op jit(solution)/shard_map/ppermute | solution.py:49
  195.0 0.8 copy-start.15
  195.8 10.6 %collective-permute-start.12 = (bf16[128,2304]{1,0:T(8,128)(2,1)S(1)}, bf16[128,2304]{1,0:T(8,128)(2,1)}, u32[]{:S(2)}, u32[]{:S(2)}) collective-permute-start(bf16[128,2304]{1,0:T(8,128)(2,1)S(1)} %collective-permute-done.11), channel_id=1, source_target_pairs={{0,1},{1,2},{2,3},{3,4},{4,5},{5,6},{6,7},{7,8},{8,9},{9,10},{10,1... | collective-permute-start | bytes 1769480 | tf_op jit(solution)/shard_map/ppermute | solution.py:49
  206.4 10.8 %collective-permute-start.13 = (bf16[128,2304]{1,0:T(8,128)(2,1)}, bf16[128,2304]{1,0:T(8,128)(2,1)}, u32[]{:S(2)}, u32[]{:S(2)}) collective-permute-start(bf16[128,2304]{1,0:T(8,128)(2,1)} %collective-permute-done.12), channel_id=1, source_target_pairs={{0,1},{1,2},{2,3},{3,4},{4,5},{5,6},{6,7},{7,8},{8,9},{9,10},{10,1... | collective-permute-start | bytes 1769480 | tf_op jit(solution)/shard_map/ppermute | solution.py:49
  217.2 11.1 %collective-permute-start.14 = (bf16[128,2304]{1,0:T(8,128)(2,1)}, bf16[128,2304]{1,0:T(8,128)(2,1)}, u32[]{:S(2)}, u32[]{:S(2)}) collective-permute-start(bf16[128,2304]{1,0:T(8,128)(2,1)} %collective-permute-done.13), channel_id=1, source_target_pairs={{0,1},{1,2},{2,3},{3,4},{4,5},{5,6},{6,7},{7,8},{8,9},{9,10},{10,1... | collective-permute-start | bytes 1769480 | tf_op jit(solution)/shard_map/ppermute | solution.py:49
  221.4 51.8 %all-to-all-start = ((bf16[16,32,2048]{2,1,0:T(8,128)(2,1)}), bf16[16,32,2048]{2,1,0:T(8,128)(2,1)}, u32[]{:S(2)}, u32[]{:S(2)}) async-start(bf16[16,32,2048]{2,1,0:T(8,128)(2,1)} %bitcast.5), calls=%async_computation | async-start | bytes 4194304 | tf_op jit(solution)/shard_map/all_to_all | solution.py:87
  228.3 10.7 %collective-permute-start.15 = (bf16[128,2304]{1,0:T(8,128)(2,1)}, bf16[128,2304]{1,0:T(8,128)(2,1)S(1)}, u32[]{:S(2)}, u32[]{:S(2)}) collective-permute-start(bf16[128,2304]{1,0:T(8,128)(2,1)} %collective-permute-done.14), channel_id=1, source_target_pairs={{0,1},{1,2},{2,3},{3,4},{4,5},{5,6},{6,7},{7,8},{8,9},{9,10},{10,1... | collective-permute-start | bytes 1769480 | tf_op jit(solution)/shard_map/ppermute | solution.py:49
  228.5 24.9 %copy-start.8 = (bf16[128,2304]{1,0:T(8,128)(2,1)S(1)}, bf16[128,2304]{1,0:T(8,128)(2,1)}, u32[]{:S(2)}) copy-start(bf16[128,2304]{1,0:T(8,128)(2,1)} %copy-done.7) | copy-start | bytes 1769476
  228.5 25.8 %copy-start.6 = (bf16[128,2304]{1,0:T(8,128)(2,1)S(1)}, bf16[128,2304]{1,0:T(8,128)(2,1)}, u32[]{:S(2)}) copy-start(bf16[128,2304]{1,0:T(8,128)(2,1)} %copy-done.5) | copy-start | bytes 1769476
  231.9 23.3 %copy-start.4 = (bf16[128,2304]{1,0:T(8,128)(2,1)S(1)}, bf16[128,2304]{1,0:T(8,128)(2,1)}, u32[]{:S(2)}) copy-start(bf16[128,2304]{1,0:T(8,128)(2,1)} %copy-done.3) | copy-start | bytes 1769476
  254.3 12.8 %copy-start.16 = (bf16[128,2304]{1,0:T(8,128)(2,1)S(1)}, bf16[128,2304]{1,0:T(8,128)(2,1)}, u32[]{:S(2)}) copy-start(bf16[128,2304]{1,0:T(8,128)(2,1)} %copy-done.15) | copy-start | bytes 1769476
  255.2 12.8 %copy-start.14 = (bf16[128,2304]{1,0:T(8,128)(2,1)S(1)}, bf16[128,2304]{1,0:T(8,128)(2,1)}, u32[]{:S(2)}) copy-start(bf16[128,2304]{1,0:T(8,128)(2,1)} %copy-done.13) | copy-start | bytes 1769476
  256.0 12.8 %copy-start.12 = (bf16[128,2304]{1,0:T(8,128)(2,1)S(1)}, bf16[128,2304]{1,0:T(8,128)(2,1)}, u32[]{:S(2)}) copy-start(bf16[128,2304]{1,0:T(8,128)(2,1)} %copy-done.11) | copy-start | bytes 1769476
  256.9 12.9 %copy-start.10 = (bf16[128,2304]{1,0:T(8,128)(2,1)S(1)}, bf16[128,2304]{1,0:T(8,128)(2,1)}, u32[]{:S(2)}) copy-start(bf16[128,2304]{1,0:T(8,128)(2,1)} %copy-done.9) | copy-start | bytes 1769476
  273.2 26.2 %all-to-all-start.2 = ((bf16[16,32,2048]{2,1,0:T(8,128)(2,1)}), bf16[16,32,2048]{2,1,0:T(8,128)(2,1)}, u32[]{:S(2)}, u32[]{:S(2)}) async-start(bf16[16,32,2048]{2,1,0:T(8,128)(2,1)} %bitcast.66), calls=%async_computation.2 | async-start | bytes 4194304 | tf_op jit(solution)/shard_map/all_to_all | solution.py:87
  280.4 137.8 %reduce-scatter.4.cloned.1.call-start = ((), (), s32[]{:S(2)}) async-start(), calls=%async_computation.5 | async-start | bytes 10027008
  308.5 4.3 copy-start.22
  308.5 7.7 %copy-start.17 = (bf16[512,768]{1,0:T(8,128)(2,1)}, bf16[512,768]{1,0:T(8,128)(2,1)S(1)}, u32[]{:S(2)}) copy-start(bf16[512,768]{1,0:T(8,128)(2,1)S(1)} %get-tuple-element.26) | copy-start | bytes 2359300
  308.5 7.7 %copy-start.20 = (bf16[512,768]{1,0:T(8,128)(2,1)}, bf16[512,768]{1,0:T(8,128)(2,1)S(1)}, u32[]{:S(2)}) copy-start(bf16[512,768]{1,0:T(8,128)(2,1)S(1)} %get-tuple-element.25) | copy-start | bytes 2359300
  337.2 1.1 copy-start.18
  338.4 3.8 copy-start.21
  342.2 12.7 %copy-start.23 = (bf16[512,768]{1,0:T(8,128)(2,1)S(1)}, bf16[512,768]{1,0:T(8,128)(2,1)}, u32[]{:S(2)}) copy-start(bf16[512,768]{1,0:T(8,128)(2,1)} %copy-done.22) | copy-start | bytes 2359300
  347.3 25.6 %all-to-all-start.3 = ((bf16[16,32,2048]{2,1,0:T(8,128)(2,1)}), bf16[16,32,2048]{2,1,0:T(8,128)(2,1)S(1)}, u32[]{:S(2)}, u32[]{:S(2)}) async-start(bf16[16,32,2048]{2,1,0:T(8,128)(2,1)} %bitcast.68), calls=%async_computation.3 | async-start | bytes 4194304 | tf_op jit(solution)/shard_map/all_to_all | solution.py:87
  372.9 10.7 %copy-start.2 = (bf16[16,32,2048]{2,1,0:T(8,128)(2,1)}, bf16[16,32,2048]{2,1,0:T(8,128)(2,1)S(1)}, u32[]{:S(2)}) copy-start(bf16[16,32,2048]{2,1,0:T(8,128)(2,1)S(1)} %all-to-all-done.3) | copy-start | bytes 6291460
  372.9 49.4 %all-to-all-start.1 = ((bf16[16,32,2048]{2,1,0:T(8,128)(2,1)}), bf16[16,32,2048]{2,1,0:T(8,128)(2,1)}, u32[]{:S(2)}, u32[]{:S(2)}) async-start(bf16[16,32,2048]{2,1,0:T(8,128)(2,1)} %bitcast.67), calls=%async_computation.1 | async-start | bytes 4194304 | tf_op jit(solution)/shard_map/all_to_all | solution.py:87
  384.2 106.0 %copy-start.1 = (bf16[1,2048,768]{2,1,0:T(8,128)(2,1)S(1)}, bf16[1,2048,768]{2,1,0:T(8,128)(2,1)}, u32[]{:S(2)}) copy-start(bf16[1,2048,768]{2,1,0:T(8,128)(2,1)} %param.11) | copy-start | bytes 9437188
  420.3 64.6 %collective-permute-start.16 = (bf16[128,2304]{0,1:T(8,128)(2,1)}, bf16[128,2304]{0,1:T(8,128)(2,1)}, u32[]{:S(2)}, u32[]{:S(2)}) collective-permute-start(bf16[128,2304]{0,1:T(8,128)(2,1)} %copy.26), channel_id=1, source_target_pairs={{0,0},{1,16},{2,32},{3,48},{4,64},{5,80},{6,96},{7,112},{8,128},{9... | collective-permute-start | bytes 1769480 | tf_op jit(solution)/shard_map/ppermute | solution.py:114
Sparse Core Ops, SparseCore 0:
  337.4 80.7 reduce-scatter.3
